TPU v7x, 32 devices: a whole 2x2x4 slice. The times are simulated.
32 devices in a mesh: dp: 8 (over z, x), mp: 4 (over y, core).
Axes of the slice: x: 2, y: 2, z: 4, core: 2. Of those that a mesh axis runs over, the one named last changes fastest.
Arguments:
- features: bfloat16 [4096, 4096], P('dp', 'mp'), may hold values from -12 to 12
- out_grad: bfloat16 [4096, 14336], P('dp', 'mp'), may hold values from -0.09375 to 0.09375
- sketch: float32 [14336, 256], P('mp'), may hold values from -0.046875 to 0.046875
Outputs:
- projector: float32 [4096, 256], P('mp')
- projected: float32 [256, 14336], P('dp', 'mp')
All inputs are finite; a program needn't handle non-finite values.
Results may differ from a plain program's by a relative error of at most 0.00055.
Values sent between devices are 32-bit elements; how exact they have to be, the bound alone decides.
A program may use at most 64 MiB of HBM per device.

v0:
```python
import jax
import jax.numpy as jnp
from jax import lax
from jax.sharding import PartitionSpec as P


def solve_panel(panel, gram_sum):
    factor = jnp.linalg.cholesky(gram_sum)
    return lax.linalg.triangular_solve(factor, panel, left_side=False, lower=True, transpose_a=True)


def orthonormal(partial_value, passes):
    highest = lax.Precision.HIGHEST
    panel = lax.psum(partial_value, "dp")
    for turn in range(passes):
        gram_sum = lax.psum(
            jnp.dot(panel.T, panel, precision=highest, preferred_element_type=jnp.float32), "mp"
        )
        panel = solve_panel(panel, gram_sum)
    return panel


def over_hidden(partial_value):
    return lax.psum(partial_value, "mp")


def per_device(features, out_grad, sketch):
    highest = lax.Precision.HIGHEST
    sketched = over_hidden(
        jnp.dot(out_grad, sketch, precision=highest, preferred_element_type=jnp.float32)
    )
    panel_one = jnp.einsum(
        "tm,tr->mr", features, sketched, precision=highest, preferred_element_type=jnp.float32
    )
    basis = orthonormal(panel_one, 1)
    image = over_hidden(
        jnp.dot(features, basis, precision=highest, preferred_element_type=jnp.float32)
    )
    columns = out_grad
    wide_share = lax.psum_scatter(
        jnp.einsum(
            "tf,tr->fr", columns, image, precision=highest, preferred_element_type=jnp.float32
        ),
        "dp",
        scatter_dimension=0,
        tiled=True,
    )
    columns = out_grad
    second_part = jnp.dot(
        columns,
        lax.all_gather(wide_share, "dp", axis=0, tiled=True),
        precision=highest,
        preferred_element_type=jnp.float32,
    )
    second = over_hidden(second_part)
    panel_two = jnp.einsum(
        "tm,tr->mr", features, second, precision=highest, preferred_element_type=jnp.float32
    )
    projector = orthonormal(panel_two, 2)
    mapped = over_hidden(
        jnp.dot(features, projector, precision=highest, preferred_element_type=jnp.float32)
    )
    projected = lax.psum_scatter(
        jnp.einsum(
            "tr,tf->rf", mapped, out_grad, precision=highest, preferred_element_type=jnp.float32
        ),
        "dp",
        scatter_dimension=0,
        tiled=True,
    )
    return (projector, projected)


def solution(mesh):
    return jax.shard_map(
        per_device,
        mesh=mesh,
        in_specs=(P("dp", "mp"), P("dp", "mp"), P("mp", None)),
        out_specs=(P("mp", None), P("dp", "mp")),
        check_vma=False,
    )
```

profile of v0, /device:TPU:0, one launch (start us, length us, event | category | flops | bytes accessed | tf_op | source)
XLA Modules:
  0.0 880.4 jit_solution(5127560758654655611)
XLA Ops:
  14.4 36.0 %all-reduce.11.cloned.1.call-done = f32[512,256]{1,0:T(8,128)} async-done(((f32[512,256]{1,0:T(8,128)}), f32[512,256]{1,0:T(8,128)}) %all-reduce.11.cloned.1.call-update) | async-done | bytes 524304 | tf_op jit(solution)/shard_map/psum | solution.py:24
  53.5 79.0 %all-reduce.13.cloned.1.call-done = f32[1024,256]{0,1:T(8,128)} async-done(((f32[1024,256]{0,1:T(8,128)}), f32[1024,256]{0,1:T(8,128)}) %all-reduce.13.cloned.1.call-update) | async-done | bytes 1048592 | tf_op jit(solution)/shard_map/psum | solution.py:14
  136.2 31.5 %all-reduce.15.cloned.1.call-done = f32[256,256]{0,1:T(8,128)} async-done(((f32[256,256]{0,1:T(8,128)}), f32[256,256]{0,1:T(8,128)}) %all-reduce.15.cloned.1.call-update) | async-done | bytes 262160 | tf_op jit(solution)/shard_map/psum | solution.py:16
  169.7 11.7 %cholesky.172 = f32[128,128]{1,0:T(8,128)S(1)} custom-call(f32[128,128]{1,0:T(8,128)S(1)} %cholesky.270), custom_call_target="Cholesky" | custom-call | tf_op jit(solution)/shard_map/jit(cholesky)/cholesky | solution.py:8
  181.5 9.8 %custom-call.15 = f32[1,128,128]{1,2,0:T(8,128)S(1)} custom-call(f32[1,128,128]{2,1,0:T(8,128)S(1)} %get-tuple-element.72), custom_call_target="InvertDiagBlocksLowerTriangular" | custom-call | tf_op jit(solution)/shard_map/jit(cholesky)/cholesky | solution.py:8
  191.8 11.7 %cholesky.189 = f32[128,128]{1,0:T(8,128)S(1)} custom-call(f32[128,128]{1,0:T(8,128)S(1)} %convolution_subtract_fusion.5), custom_call_target="Cholesky" | custom-call | tf_op jit(solution)/shard_map/jit(cholesky)/cholesky | solution.py:8
  209.6 19.7 %custom-call.16 = f32[2,128,128]{1,2,0:T(8,128)S(1)} custom-call(f32[2,128,128]{2,1,0:T(8,128)S(1)} %get-tuple-element.24), custom_call_target="InvertDiagBlocksLowerTriangular" | custom-call | tf_op jit(solution)/shard_map/triangular_solve/custom-call.0 | solution.py:9
  233.1 33.3 %all-reduce.17.cloned.1.call-done = f32[512,256]{0,1:T(8,128)} async-done(((f32[512,256]{0,1:T(8,128)}), f32[512,256]{0,1:T(8,128)}) %all-reduce.17.cloned.1.call-update) | async-done | bytes 524304 | tf_op jit(solution)/shard_map/psum | solution.py:24
  278.6 81.0 %reduce-scatter.7.cloned.1.call-done = f32[448,256]{1,0:T(8,128)} async-done(((f32[3584,256]{1,0:T(8,128)}), f32[448,256]{1,0:T(8,128)}) %reduce-scatter.7.cloned.1.call-update) | async-done | bytes 458768 | tf_op jit(solution)/shard_map/reduce_scatter | solution.py:40
  360.2 68.1 %all-gather.2.cloned.1.call-done = f32[3584,256]{1,0:T(8,128)} async-done(((f32[448,256]{1,0:T(8,128)}), f32[3584,256]{1,0:T(8,128)}) %all-gather.2.cloned.1.call-update) | async-done | bytes 3670032 | tf_op jit(solution)/shard_map/all_gather | solution.py:51
  428.3 9.8 %convolution_bitcast_fusion.5 = f32[512,256]{0,1:T(8,128)} fusion(f32[3584,256]{1,0:T(8,128)} %all-gather.2.cloned.1.call-done, bf16[512,3584]{1,0:T(8,128)(2,1)} %param.7), kind=kOutput, calls=%fused_computation.11 | convolution fusion | flops 5637144576 | bytes 7864320 | tf_op jit(solution)/shard_map/dot_general | solution.py:49
  438.2 31.8 %all-reduce.19.cloned.1.call-done = f32[512,256]{0,1:T(8,128)} async-done(((f32[512,256]{0,1:T(8,128)}), f32[512,256]{0,1:T(8,128)}) %all-reduce.19.cloned.1.call-update) | async-done | bytes 524304 | tf_op jit(solution)/shard_map/psum | solution.py:24
  473.0 79.0 %all-reduce.21.cloned.1.call-done = f32[1024,256]{0,1:T(8,128)} async-done(((f32[1024,256]{0,1:T(8,128)}), f32[1024,256]{0,1:T(8,128)}) %all-reduce.21.cloned.1.call-update) | async-done | bytes 1048592 | tf_op jit(solution)/shard_map/psum | solution.py:14
  555.6 31.5 %all-reduce.23.cloned.1.call-done = f32[256,256]{0,1:T(8,128)} async-done(((f32[256,256]{0,1:T(8,128)}), f32[256,256]{0,1:T(8,128)}) %all-reduce.23.cloned.1.call-update) | async-done | bytes 262160 | tf_op jit(solution)/shard_map/psum | solution.py:16
  589.2 11.7 %cholesky.206 = f32[128,128]{1,0:T(8,128)S(1)} custom-call(f32[128,128]{1,0:T(8,128)S(1)} %cholesky.273), custom_call_target="Cholesky" | custom-call | tf_op jit(solution)/shard_map/jit(cholesky)/cholesky | solution.py:8
  601.0 9.8 %custom-call.17 = f32[1,128,128]{1,2,0:T(8,128)S(1)} custom-call(f32[1,128,128]{2,1,0:T(8,128)S(1)} %get-tuple-element.68), custom_call_target="InvertDiagBlocksLowerTriangular" | custom-call | tf_op jit(solution)/shard_map/jit(cholesky)/cholesky | solution.py:8
  611.3 11.7 %cholesky.223 = f32[128,128]{1,0:T(8,128)S(1)} custom-call(f32[128,128]{1,0:T(8,128)S(1)} %convolution_subtract_fusion.4), custom_call_target="Cholesky" | custom-call | tf_op jit(solution)/shard_map/jit(cholesky)/cholesky | solution.py:8
  629.6 19.7 %custom-call.18 = f32[2,128,128]{1,2,0:T(8,128)S(1)} custom-call(f32[2,128,128]{2,1,0:T(8,128)S(1)} %get-tuple-element.25), custom_call_target="InvertDiagBlocksLowerTriangular" | custom-call | tf_op jit(solution)/shard_map/triangular_solve/custom-call.0 | solution.py:9
  653.0 32.1 %all-reduce.25.cloned.1.call-done = f32[256,256]{0,1:T(8,128)} async-done(((f32[256,256]{0,1:T(8,128)}), f32[256,256]{0,1:T(8,128)}) %all-reduce.25.cloned.1.call-update) | async-done | bytes 262160 | tf_op jit(solution)/shard_map/psum | solution.py:16
  687.2 11.7 %cholesky.240 = f32[128,128]{1,0:T(8,128)S(1)} custom-call(f32[128,128]{1,0:T(8,128)S(1)} %cholesky.276), custom_call_target="Cholesky" | custom-call | tf_op jit(solution)/shard_map/jit(cholesky)/cholesky | solution.py:8
  709.3 11.7 %cholesky.257 = f32[128,128]{1,0:T(8,128)S(1)} custom-call(f32[128,128]{1,0:T(8,128)S(1)} %convolution_subtract_fusion.3), custom_call_target="Cholesky" | custom-call | tf_op jit(solution)/shard_map/jit(cholesky)/cholesky | solution.py:8
  727.9 19.7 %custom-call.20 = f32[2,128,128]{1,2,0:T(8,128)S(1)} custom-call(f32[2,128,128]{2,1,0:T(8,128)S(1)} %get-tuple-element.26), custom_call_target="InvertDiagBlocksLowerTriangular" | custom-call | tf_op jit(solution)/shard_map/triangular_solve/custom-call.0 | solution.py:9
  751.3 33.3 %all-reduce.27.cloned.1.call-done = f32[512,256]{0,1:T(8,128)} async-done(((f32[512,256]{0,1:T(8,128)}), f32[512,256]{0,1:T(8,128)}) %all-reduce.27.cloned.1.call-update) | async-done | bytes 524304 | tf_op jit(solution)/shard_map/psum | solution.py:24
  793.1 80.0 %reduce-scatter.5.cloned.1.call-done = f32[32,3584]{1,0:T(8,128)} async-done(((f32[256,3584]{1,0:T(8,128)}), f32[32,3584]{1,0:T(8,128)}) %reduce-scatter.5.cloned.1.call-update) | async-done | bytes 458768 | tf_op jit(solution)/shard_map/reduce_scatter | solution.py:63
  (111 shorter events, 98.0 us)
Async XLA Ops:
  7.2 43.3 %copy-start = (bf16[512,1024]{1,0:T(8,128)(2,1)S(1)}, bf16[512,1024]{1,0:T(8,128)(2,1)}, u32[]{:S(2)}) copy-start(bf16[512,1024]{1,0:T(8,128)(2,1)} %param.6) | copy-start | bytes 3145732
  7.2 43.3 %all-reduce.11.cloned.1.call-start = ((), (), s32[]{:S(2)}) async-start(), calls=%async_computation.2 | async-start | bytes 1048576 | tf_op jit(solution)/shard_map/psum | solution.py:24
  14.4 118.1 %all-reduce.13.cloned.1.call-start = ((), (), s32[]{:S(2)}) async-start(), calls=%async_computation.3 | async-start | bytes 2097152 | tf_op jit(solution)/shard_map/psum | solution.py:14
  53.5 114.1 %all-reduce.15.cloned.1.call-start = ((), (), s32[]{:S(2)}) async-start(), calls=%async_computation.4 | async-start | bytes 524288 | tf_op jit(solution)/shard_map/psum | solution.py:16
  132.5 96.8 %copy-start.1 = (f32[1024,256]{0,1:T(8,128)S(1)}, f32[1024,256]{0,1:T(8,128)}, u32[]{:S(2)}) copy-start(f32[1024,256]{0,1:T(8,128)} %all-reduce.13.cloned.1.call-done) | copy-start | bytes 3145732
  135.9 130.5 %all-reduce.17.cloned.1.call-start = ((), (), s32[]{:S(2)}) async-start(), calls=%async_computation.5 | async-start | bytes 1048576 | tf_op jit(solution)/shard_map/psum | solution.py:24
  233.0 126.6 %reduce-scatter.7.cloned.1.call-start = ((), (), s32[]{:S(2)}) async-start(), calls=%async_computation.13 | async-start | bytes 4128768 | tf_op jit(solution)/shard_map/reduce_scatter | solution.py:40
  278.6 149.7 %all-gather.2.cloned.1.call-start = ((), (), s32[]{:S(2)}) async-start(), calls=%async_computation.6 | async-start | bytes 4128768 | tf_op jit(solution)/shard_map/all_gather | solution.py:51
  359.7 110.3 %all-reduce.19.cloned.1.call-start = ((), (), s32[]{:S(2)}) async-start(), calls=%async_computation.7 | async-start | bytes 1048576 | tf_op jit(solution)/shard_map/psum | solution.py:24
  438.1 113.9 %all-reduce.21.cloned.1.call-start = ((), (), s32[]{:S(2)}) async-start(), calls=%async_computation.8 | async-start | bytes 2097152 | tf_op jit(solution)/shard_map/psum | solution.py:14
  473.0 114.2 %all-reduce.23.cloned.1.call-start = ((), (), s32[]{:S(2)}) async-start(), calls=%async_computation.9 | async-start | bytes 524288 | tf_op jit(solution)/shard_map/psum | solution.py:16
  552.0 97.3 %copy-start.2 = (f32[1024,256]{0,1:T(8,128)S(1)}, f32[1024,256]{0,1:T(8,128)}, u32[]{:S(2)}) copy-start(f32[1024,256]{0,1:T(8,128)} %all-reduce.21.cloned.1.call-done) | copy-start | bytes 3145732
  555.4 129.7 %all-reduce.25.cloned.1.call-start = ((), (), s32[]{:S(2)}) async-start(), calls=%async_computation.10 | async-start | bytes 524288 | tf_op jit(solution)/shard_map/psum | solution.py:16
  653.0 131.6 %all-reduce.27.cloned.1.call-start = ((), (), s32[]{:S(2)}) async-start(), calls=%async_computation.11 | async-start | bytes 1048576 | tf_op jit(solution)/shard_map/psum | solution.py:24
  751.3 121.8 %reduce-scatter.5.cloned.1.call-start = ((), (), s32[]{:S(2)}) async-start(), calls=%async_computation.12 | async-start | bytes 4128768 | tf_op jit(solution)/shard_map/reduce_scatter | solution.py:63
Sparse Core Ops, SparseCore 0:
  14.5 35.8 all-reduce.10
  54.5 77.9 all-reduce.12
  136.0 31.5 all-reduce.14
  233.1 33.1 all-reduce.16
  278.7 80.9 reduce-scatter.6
  361.7 66.5 all-gather.1
  438.2 31.6 all-reduce.18
  474.0 77.9 all-reduce.20
  555.5 31.5 all-reduce.22
  653.1 31.9 all-reduce.24
  751.4 33.1 all-reduce.26
  791.8 81.2 reduce-scatter.4
where the time goes:
time: 885 us; the launch traced here: 880 us
  waiting for transfers between devices  617 us (70%)
  other arithmetic  165 us (19%)
  matrix products  56.1 us (6%)
  local copies, waits for them, and re-layouts  21.4 us (2%)
  between operations  18.7 us (2%)
    psum x2, waiting for transfers between devices, orthonormal(): panel = lax.psum(partial_value, 'dp')  158 us
    psum x4, waiting for transfers between devices, over_hidden(): return lax.psum(partial_value, 'mp')  134 us
    another operation x20, other arithmetic, solve_panel(): factor = jnp.linalg.cholesky(gram_sum)  103 us
    psum x3, waiting for transfers between devices, orthonormal(): lax.psum(jnp.dot(panel.T, panel, precision=highest, preferred_element_typ...  95 us
    reduce_scatter x1, waiting for transfers between devices, per_device(): lax.psum_scatter(jnp.einsum('tf,tr->fr', columns, image, precision=highes...  81 us
    reduce_scatter x1, waiting for transfers between devices, per_device(): lax.psum_scatter(jnp.einsum('tr,tf->rf', mapped, out_grad, precision=high...  80 us
    all_gather x1, waiting for transfers between devices, per_device(): lax.all_gather(wide_share, 'dp', axis=0, tiled=True)  68.1 us
    another operation x8, other arithmetic, solve_panel(): lax.linalg.triangular_solve(factor, panel, left_side=False, lower=True, t...  59.2 us
  transfers between devices with their start and end apart: 12, of which 12 were waited for; matrix products, arithmetic and copies ran while one was open for 0% of the time, Pallas kernels for 0%

commit v1 on v0

v1 whole, which is shorter than its diff:
```python
import functools

import jax
import jax.numpy as jnp
from jax import lax
from jax.experimental import pallas as pl
from jax.experimental.pallas import tpu as pltpu
from jax.sharding import PartitionSpec as P

F32 = jnp.float32
HIGHEST = lax.Precision.HIGHEST
VMEM = pl.BlockSpec(memory_space=pltpu.VMEM)
BLOCK = 128


def sum_kernel(axis, n, gather, x_ref, out_ref, near, total, far, sems):
    groups = n // 2
    me = lax.axis_index(axis)
    parity = lax.rem(me, 2)
    group = lax.div(me, 2)
    mate = me + 1 - 2 * parity

    def member(k):
        return lax.rem(group + k, groups)

    def send(src, dst, row, slot, target):
        copy = pltpu.make_async_remote_copy(
            src_ref=src,
            dst_ref=dst,
            send_sem=sems.at[2 * row, slot],
            recv_sem=sems.at[2 * row + 1, slot],
            device_id={axis: target},
            device_id_type=pl.DeviceIdType.MESH,
        )
        copy.start()
        return copy

    barrier = pltpu.get_barrier_semaphore()
    pl.semaphore_signal(barrier, inc=1, device_id={axis: mate}, device_id_type=pl.DeviceIdType.MESH)
    for k in range(1, groups):
        pl.semaphore_signal(
            barrier, inc=1, device_id={axis: 2 * member(k) + parity}, device_id_type=pl.DeviceIdType.MESH
        )
    pl.semaphore_wait(barrier, groups)

    order = list(range(1, groups)) + [0]
    first = {k: send(x_ref.at[2 * member(k) + 1 - parity], near.at[k], 0, k, mate) for k in order}
    second = {}
    for k in order:
        first[k].wait_recv()
        total[k] = x_ref[2 * member(k) + parity] + near[k]
        if k:
            second[k] = send(total.at[k], far.at[k - 1], 1, k, 2 * member(k) + parity)
    mine = total[0]
    for k in range(1, groups):
        second[k].wait_recv()
        mine = mine + far[k - 1]
    copies = list(first.values()) + list(second.values())
    waits = []
    if gather:
        out_ref[me] = mine
        across = [send(out_ref.at[me], out_ref.at[me], 2, k, 2 * member(k) + parity) for k in range(1, groups)]
        side = [send(out_ref.at[me], out_ref.at[me], 3, 0, mate)]
        for k in range(1, groups):
            across[k - 1].wait_recv()
            block = out_ref.at[2 * member(groups - k) + parity]
            side.append(send(block, block, 3, k, mate))
        for copy in side:
            copy.wait_recv()
        copies += across + side
    else:
        out_ref[...] = mine
    for copy in copies:
        copy.wait_send()


def summed(x, axis, n, ident, gather=True):
    rows, columns = x.shape
    piece = rows // n
    groups = n // 2
    size = 4 * rows * columns
    out = pl.pallas_call(
        functools.partial(sum_kernel, axis, n, gather),
        out_shape=jax.ShapeDtypeStruct((n, piece, columns) if gather else (piece, columns), F32),
        in_specs=[VMEM],
        out_specs=VMEM,
        scratch_shapes=[
            pltpu.VMEM((groups, piece, columns), F32),
            pltpu.VMEM((groups, piece, columns), F32),
            pltpu.VMEM((max(groups - 1, 1), piece, columns), F32),
            pltpu.SemaphoreType.DMA((8, groups)),
        ],
        compiler_params=pltpu.CompilerParams(
            collective_id=ident, has_side_effects=True, vmem_limit_bytes=6 * size + (8 << 20)
        ),
    )(x.reshape(n, piece, columns))
    return out.reshape(rows, columns) if gather else out


def inverse_factor(a):
    tiles = BLOCK // 8
    sub = lax.broadcasted_iota(jnp.int32, (8, 1), 0)
    lane = lax.broadcasted_iota(jnp.int32, (8, BLOCK), 1)
    eye_row = lax.broadcasted_iota(jnp.int32, (8, BLOCK), 0)
    left = [a[8 * i : 8 * i + 8, :] for i in range(tiles)]
    right = [jnp.where(lane == eye_row + 8 * i, 1.0, 0.0).astype(F32) for i in range(tiles)]
    pivots = [jnp.ones((8, 1), F32) for _ in range(tiles)]
    for j in range(BLOCK):
        t, s = j // 8, j % 8
        row = left[t][s : s + 1, :]
        pivot = row[:, j : j + 1]
        scale = 1.0 / pivot
        pivots[t] = jnp.where(sub == s, pivot, pivots[t])
        row = row * scale
        other = right[t][s : s + 1, :] * scale
        for i in range(t, tiles):
            if i == t and s == 7:
                continue
            col = left[i][:, j : j + 1]
            if i == t:
                col = jnp.where(sub > s, col, 0.0)
            left[i] = left[i] - col * row
            right[i] = right[i] - col * other
    return jnp.concatenate([right[i] * (1.0 / jnp.sqrt(pivots[i])) for i in range(tiles)], axis=0)


def dot(a, b, dims=((1,), (0,))):
    return lax.dot_general(a, b, (dims, ((), ())), precision=HIGHEST, preferred_element_type=F32)


def solve_kernel(count, gram_ref, *refs):
    inv, low, rest = refs[-3:]
    blocks = gram_ref.shape[0] // BLOCK
    rest[...] = gram_ref[...]
    inv[...] = jnp.zeros_like(inv)

    @pl.loop(0, blocks)
    def _(b):
        at = pl.ds(pl.multiple_of(b * BLOCK, BLOCK), BLOCK)
        w = inverse_factor(rest[at, at])
        low[...] = dot(rest[:, at], w, ((1,), (1,)))
        rest[...] = rest[...] - dot(low[...], low[...], ((1,), (1,)))
        inv[at, at] = w

    gram = gram_ref[...]
    for i in range(1, blocks):
        here = slice(i * BLOCK, (i + 1) * BLOCK)
        done = inv[0 : i * BLOCK, 0 : i * BLOCK]
        w = inv[here, here]
        factor = dot(gram[here, 0 : i * BLOCK], done, ((1,), (1,)))
        inv[here, 0 : i * BLOCK] = -dot(w, dot(factor, done))
    for index in range(count):
        refs[count + index][...] = dot(refs[index][...], inv[...], ((1,), (1,)))


def solved(gram, *panels):
    rank = gram.shape[0]
    return pl.pallas_call(
        functools.partial(solve_kernel, len(panels)),
        out_shape=[jax.ShapeDtypeStruct(p.shape, F32) for p in panels],
        in_specs=[VMEM] * (1 + len(panels)),
        out_specs=[VMEM] * len(panels),
        scratch_shapes=[
            pltpu.VMEM((rank, rank), F32),
            pltpu.VMEM((rank, BLOCK), F32),
            pltpu.VMEM((rank, rank), F32),
        ],
        compiler_params=pltpu.CompilerParams(vmem_limit_bytes=32 << 20),
    )(gram, *panels)


def pieces(value):
    terms = []
    for _ in range(3):
        term = lax.reduce_precision(value, 8, 7)
        terms.append(term.astype(jnp.bfloat16))
        value = value - term
    return terms


def exact_dot(a, b, contract):
    width = b.shape[1]
    c = lax.dot_general(
        a,
        jnp.concatenate(pieces(b), axis=1),
        (((contract,), (0,)), ((), ())),
        preferred_element_type=F32,
    )
    return c[:, :width] + (c[:, width : 2 * width] + c[:, 2 * width :])


def per_device(dp, mp, features, out_grad, sketch):
    tokens = features.shape[0]
    rank = sketch.shape[1]
    sketched = summed(exact_dot(out_grad, sketch, 1), "mp", mp, 0)
    panel = summed(exact_dot(features, sketched, 0), "dp", dp, 1)
    both = summed(
        jnp.concatenate([exact_dot(features, panel, 1), dot(panel, panel, ((0,), (0,)))]), "mp", mp, 2
    )
    (image,) = solved(both[tokens:], both[:tokens])
    wide = summed(exact_dot(out_grad, image, 0), "dp", dp, 3)
    second = summed(exact_dot(out_grad, wide, 1), "mp", mp, 4)
    panel = summed(exact_dot(features, second, 0), "dp", dp, 5)
    (panel,) = solved(summed(dot(panel, panel, ((0,), (0,))), "mp", mp, 6), panel)
    both = summed(
        jnp.concatenate([exact_dot(features, panel, 1), dot(panel, panel, ((0,), (0,)))]), "mp", mp, 7
    )
    projector, mapped = solved(both[tokens:], panel, both[:tokens])
    terms = jnp.concatenate(pieces(mapped), axis=1)
    c = lax.dot_general(terms, out_grad, (((0,), (0,)), ((), ())), preferred_element_type=F32)
    share = c[:rank] + (c[rank : 2 * rank] + c[2 * rank :])
    return (projector, summed(share, "dp", dp, 8, gather=False))


def solution(mesh):
    return jax.shard_map(
        functools.partial(per_device, mesh.shape["dp"], mesh.shape["mp"]),
        mesh=mesh,
        in_specs=(P("dp", "mp"), P("dp", "mp"), P("mp", None)),
        out_specs=(P("mp", None), P("dp", "mp")),
        check_vma=False,
    )
```

time: 885 us -> 446 us (0.50)
  waiting for transfers between devices: 617 us -> 0 us
  Pallas kernels: 0 us -> 397 us
  other arithmetic: 165 us -> 9.75 us
  matrix products: 56.1 us -> 20.8 us
  between operations: 18.7 us -> 1.52 us
  local copies, waits for them, and re-layouts: 21.4 us -> 10.5 us
    pallas_call x0 -> x12, Pallas kernels: none -> 397 us  [the longest x9 321 us: summed(): pl.pallas_call(functools.partial(sum_kernel, axis, n, gather), out_shape=...]
    psum x9 -> x0, waiting for transfers between devices: 387 us -> none  [the longest x2 158 us: orthonormal(): panel = lax.psum(partial_value, 'dp')]
    another operation x28 -> x0, other arithmetic: 162 us -> none  [the longest x20 103 us: solve_panel(): factor = jnp.linalg.cholesky(gram_sum)]
    reduce_scatter x2 -> x0, waiting for transfers between devices: 161 us -> none  [the longest x1 81 us: per_device(): lax.psum_scatter(jnp.einsum('tf,tr->fr', columns, image, precision=highes...]
    all_gather x1 -> x0, waiting for transfers between devices: 68.1 us -> none  [per_device(): lax.all_gather(wide_share, 'dp', axis=0, tiled=True)]
    dot_general x11, matrix products: 49.1 us -> 20.8 us  [the longest x7 13.1 us: exact_dot(): lax.dot_general(a, jnp.concatenate(pieces(b), axis=1), (((contract,), (0,...]
    another operation x28 -> x0, local copies, waits for them, and re-layouts: 11.7 us -> none  [the longest x22 11.6 us: solve_panel(): lax.linalg.triangular_solve(factor, panel, left_side=False, lower=True, t...]
  transfers between devices with their start and end apart: 12 -> 0, of which waited for: 12 -> 0; matrix products, arithmetic and copies ran while one was open for 0% -> 0% of each run, Pallas kernels for 0% -> 0%
where the time goes in v1:
time: 446 us; the launch traced here: 440 us
  Pallas kernels  397 us (89%)
  matrix products  20.8 us (5%)
  local copies, waits for them, and re-layouts  10.5 us (2%)
  other arithmetic  9.75 us (2%)
    pallas_call x9, Pallas kernels, summed(): pl.pallas_call(functools.partial(sum_kernel, axis, n, gather), out_shape=...  321 us
    pallas_call x3, Pallas kernels, solved(): pl.pallas_call(functools.partial(solve_kernel, len(panels)), out_shape=[j...  76.3 us
    dot_general x7, matrix products, exact_dot(): lax.dot_general(a, jnp.concatenate(pieces(b), axis=1), (((contract,), (0,...  13.1 us

profile of v1, /device:TPU:0, one launch (start us, length us, event | category | flops | bytes accessed | tf_op | source)
XLA Modules:
  0.0 439.6 jit_solution(2607028414624183873)
XLA Ops:
  0.7 3.1 reduce-precision_convert_fusion.3
  3.9 3.0 fusion.33
  7.0 14.4 %shard_map.50 = f32[4,128,256]{2,1,0:T(8,128)S(1)} custom-call(f32[4,128,256]{2,1,0:T(8,128)S(1)} %bitcast.88), custom_call_target="tpu_custom_call" | custom-call | tf_op jit(solution)/shard_map/pallas_call | solution.py:82
  23.2 37.7 %shard_map.51 = f32[8,128,256]{2,1,0:T(8,128)S(1)} custom-call(f32[8,128,256]{2,1,0:T(8,128)S(1)} %bitcast.80), custom_call_target="tpu_custom_call" | custom-call | tf_op jit(solution)/shard_map/pallas_call | solution.py:82
  61.0 1.8 convolution_bitcast_fusion.3
  64.3 15.5 %shard_map.52 = f32[4,192,256]{2,1,0:T(8,128)S(1)} custom-call(f32[4,192,256]{2,1,0:T(8,128)S(1)} %bitcast.82), custom_call_target="tpu_custom_call" | custom-call | tf_op jit(solution)/shard_map/pallas_call | solution.py:82
  79.8 24.6 %shard_map.53 = f32[512,256]{1,0:T(8,128)S(1)} custom-call(f32[256,256]{1,0:T(8,128)S(1)} %slice.121.gram_ref, f32[512,256]{1,0:T(8,128)S(1)} %slice.122.refs_0_), custom_call_target="tpu_custom_call" | custom-call | tf_op jit(solution)/shard_map/pallas_call | solution.py:158
  104.6 3.1 convolution_bitcast_fusion
  107.7 2.7 fusion.17
  110.4 5.3 %copy.12 = f32[3584,256]{1,0:T(8,128)} copy(f32[3584,256]{0,1:T(8,128)} %fusion.17) | data formatting | bytes 7340032 | tf_op jit(solution)/shard_map/add | solution.py:189
  115.8 2.0 copy-done.1
  117.8 110.0 %shard_map.54 = f32[8,448,256]{2,1,0:T(8,128)S(1)} custom-call(f32[8,448,256]{2,1,0:T(8,128)S(1)} %bitcast.78), custom_call_target="tpu_custom_call" | custom-call | tf_op jit(solution)/shard_map/pallas_call | solution.py:82
  228.8 1.0 copy-done.4
  229.9 3.0 fusion.30
  233.0 12.6 %shard_map.55 = f32[4,128,256]{2,1,0:T(8,128)S(1)} custom-call(f32[4,128,256]{2,1,0:T(8,128)S(1)} %bitcast.89), custom_call_target="tpu_custom_call" | custom-call | tf_op jit(solution)/shard_map/pallas_call | solution.py:82
  247.4 47.1 %shard_map.56 = f32[8,128,256]{2,1,0:T(8,128)S(1)} custom-call(f32[8,128,256]{2,1,0:T(8,128)S(1)} %bitcast.81), custom_call_target="tpu_custom_call" | custom-call | tf_op jit(solution)/shard_map/pallas_call | solution.py:82
  294.9 1.0 fusion.89.x_ref
  295.9 9.4 %shard_map.57 = f32[4,64,256]{2,1,0:T(8,128)S(1)} custom-call(f32[4,64,256]{2,1,0:T(8,128)S(1)} %fusion.89.x_ref), custom_call_target="tpu_custom_call" | custom-call | tf_op jit(solution)/shard_map/pallas_call | solution.py:82
  305.3 25.1 %shard_map.58.refs_0_ = f32[1024,256]{1,0:T(8,128)S(1)} custom-call(f32[256,256]{1,0:T(8,128)S(1)} %bitcast.90, f32[1024,256]{1,0:T(8,128)S(1)} %bitcast.77), custom_call_target="tpu_custom_call" | custom-call | tf_op jit(solution)/shard_map/pallas_call | solution.py:158
  330.4 1.8 fusion.90
  333.7 15.6 %shard_map.59 = f32[4,192,256]{2,1,0:T(8,128)S(1)} custom-call(f32[4,192,256]{2,1,0:T(8,128)S(1)} %bitcast.85), custom_call_target="tpu_custom_call" | custom-call | tf_op jit(solution)/shard_map/pallas_call | solution.py:82
  349.3 26.6 %shard_map.60 = (f32[1024,256]{1,0:T(8,128)}, f32[512,256]{1,0:T(8,128)S(1)}) custom-call(f32[256,256]{1,0:T(8,128)S(1)} %slice.135.gram_ref, f32[1024,256]{1,0:T(8,128)S(1)} %shard_map.58.refs_0_, f32[512,256]{1,0:T(8,128)S(1)} %slice.136.refs_1_), custom_call_target="tpu_custom_call" | custom-call | tf_op jit(solution)/shard_map/pallas_call | solution.py:158
  376.0 3.1 fusion.63
  380.0 58.3 %shard_map.61 = f32[32,3584]{1,0:T(8,128)S(1)} custom-call(f32[8,32,3584]{2,1,0:T(8,128)S(1)} %bitcast.79), custom_call_target="tpu_custom_call" | custom-call | tf_op jit(solution)/shard_map/pallas_call | solution.py:82
  (38 shorter events, 10.1 us)
Async XLA Ops:
  0.6 20.9 %copy-start = (bf16[512,1024]{1,0:T(8,128)(2,1)S(1)}, bf16[512,1024]{1,0:T(8,128)(2,1)}, u32[]{:S(2)}) copy-start(bf16[512,1024]{1,0:T(8,128)(2,1)} %param.3) | copy-start | bytes 3145732
  0.6 3.2 copy-start.2
  64.3 40.4 %copy-start.3 = (bf16[512,3584]{1,0:T(8,128)(2,1)S(1)}, bf16[512,3584]{1,0:T(8,128)(2,1)}, u32[]{:S(2)}) copy-start(bf16[512,3584]{1,0:T(8,128)(2,1)} %param.4) | copy-start | bytes 11010052
  115.7 2.0 copy-start.1
  227.8 2.0 copy-start.4
  333.7 42.3 %copy-start.5 = (bf16[512,3584]{1,0:T(8,128)(2,1)S(1)}, bf16[512,3584]{1,0:T(8,128)(2,1)}, u32[]{:S(2)}) copy-start(bf16[512,3584]{1,0:T(8,128)(2,1)} %param.4) | copy-start | bytes 11010052
